TPU v7x, 32 devices: a whole 2x2x4 slice. The times are simulated.
32 devices in a mesh: tm: 4 (over y, x), pts: 8 (over z, core).
Axes of the slice: x: 2, y: 2, z: 4, core: 2. Of those that a mesh axis runs over, the one named last changes fastest.
Arguments:
- codes: bfloat16 [11520, 5120], P('tm', 'pts'), as said below
- scales: float32 [11520], P('tm'), may hold values from 0.005 to 0.015
- weights: float32 [5120], P('pts'), may hold values from 0.5 to 4
- freq_indices: int32 [64], replicated, may hold values from 0 to 127, as said below
Outputs:
- cross_spectral: float32 [64, 2, 89, 89], P('pts')
Inputs may be any that keep to these rules, and one draw needn't show every extreme that they name: `codes`: whole numbers. `freq_indices`: distinct bins.
All inputs are finite; a program needn't handle non-finite values.
Results may differ from a plain program's by a relative error of at most 0.0011.
Values may be sent and summed in bfloat16 or wider, within the bound.
A program may use at most 64 MiB of HBM per device.

v0:
```python
import math

import jax
import jax.numpy as jnp
from jax import lax
from jax.sharding import PartitionSpec as P

NFFT = 256


def make_tables(freq_indices):
    sample = jnp.arange(NFFT, dtype=jnp.int32)
    phases = freq_indices[:, None] * sample[None, :] % NFFT
    angles = phases.astype(jnp.float32) * (2.0 * math.pi / NFFT)
    hann_window = 0.5 - 0.5 * jnp.cos(sample.astype(jnp.float32) * (2.0 * math.pi / NFFT))
    cosine_table = (0.25 * hann_window[None, :] * jnp.cos(angles)).astype(jnp.bfloat16)
    sine_table = (-0.25 * hann_window[None, :] * jnp.sin(angles)).astype(jnp.bfloat16)
    return (cosine_table, sine_table)


def cross_matrices(stacked):
    blocks = stacked.shape[1] // 2
    products = jnp.einsum("fip,fjp->fij", stacked, stacked, preferred_element_type=jnp.float32)
    matrix_re = products[:, :blocks, :blocks] + products[:, blocks:, blocks:]
    matrix_im = products[:, :blocks, blocks:] - products[:, blocks:, :blocks]
    return jnp.stack([matrix_re, matrix_im], axis=1)


def per_device(codes, scales, weights, freq_indices):
    values = (codes.astype(jnp.float32) * scales[:, None]).astype(jnp.bfloat16)
    regrouped = lax.all_to_all(values, "tm", split_axis=1, concat_axis=0, tiled=True)
    point_count = regrouped.shape[1]
    own_weights = lax.dynamic_slice_in_dim(
        weights, lax.axis_index("tm") * point_count, point_count, 0
    )
    total_points = weights.shape[0] * lax.axis_size("pts")
    root_weight = jnp.sqrt(own_weights / total_points)
    cosine_table, sine_table = make_tables(freq_indices)
    hop_rows = regrouped.reshape(-1, NFFT // 2, point_count)
    windows = jnp.concatenate([hop_rows[:-1], hop_rows[1:]], axis=1)
    real_part = jnp.einsum("fn,bnp->fbp", cosine_table, windows, preferred_element_type=jnp.float32)
    imag_part = jnp.einsum("fn,bnp->fbp", sine_table, windows, preferred_element_type=jnp.float32)
    scaled_re = (real_part * root_weight[None, None, :]).astype(jnp.bfloat16)
    scaled_im = (imag_part * root_weight[None, None, :]).astype(jnp.bfloat16)
    stacked = jnp.concatenate([scaled_re, scaled_im], axis=1)
    partial_value = lax.psum_scatter(
        cross_matrices(stacked), "pts", scatter_dimension=0, tiled=True
    )
    return lax.psum(partial_value, "tm")


def solution(mesh):
    return jax.shard_map(
        per_device,
        mesh=mesh,
        in_specs=(P("tm", "pts"), P("tm"), P("pts"), P()),
        out_specs=P("pts", None, None, None),
        check_vma=False,
    )
```

profile of v0, /device:TPU:0, one launch (start us, length us, event | category | flops | bytes accessed | tf_op | source)
XLA Modules:
  0.0 320.9 jit_solution(16545950724297518855)
XLA Ops:
  6.5 0.0 copy-start
  6.5 6.2 %copy.9 = bf16[2880,640]{0,1:T(8,128)(2,1)} copy(bf16[2880,640]{1,0:T(8,128)(2,1)} %param.4) | data formatting | bytes 7372800 | tf_op args[0]
  12.7 0.0 copy-done
  12.7 4.6 %multiply_convert_fusion = bf16[2880,640]{0,1:T(8,128)(2,1)} fusion(bf16[2880,640]{0,1:T(8,128)(2,1)} %copy.9, f32[2880]{0:T(1024)S(1)} %copy-done), kind=kLoop, calls=%fused_computation.1 | loop fusion | flops 5529600 | bytes 7384320 | tf_op jit(solution)/shard_map/convert_element_type | solution.py:30
  17.3 5.2 %all-to-all-start = ((bf16[2880,4,160]{0,2,1:T(8,128)(2,1)}), bf16[2880,4,160]{0,2,1:T(8,128)(2,1)}, u32[]{:S(2)}, u32[]{:S(2)}) async-start(bf16[2880,4,160]{0,2,1:T(8,128)(2,1)} %bitcast.15), calls=%async_computation | async-start | bytes 7536640 | tf_op jit(solution)/shard_map/all_to_all | solution.py:31
  22.5 0.0 all-reduce.6.cloned.1.call-start
  22.6 0.8 multiply_sqrt_fusion
  23.3 43.1 %all-to-all-done = bf16[2880,4,160]{0,2,1:T(8,128)(2,1)} async-done(((bf16[2880,4,160]{0,2,1:T(8,128)(2,1)}), bf16[2880,4,160]{0,2,1:T(8,128)(2,1)}, u32[]{:S(2)}, u32[]{:S(2)}) %all-to-all-start) | async-done | bytes 3686432 | tf_op jit(solution)/shard_map/all_to_all | solution.py:31
  66.4 5.9 %copy.10 = bf16[4,2880,160]{1,0,2:T(4,128)(2,1)} copy(bf16[4,2880,160]{1,2,0:T(8,128)(2,1)} %bitcast.2) | data formatting | bytes 7372800 | tf_op jit(solution)/shard_map/all_to_all | solution.py:31
  72.3 8.5 %reshape.24 = bf16[90,128,160]{1,0,2:T(8,128)(2,1)} reshape(bf16[4,2880,160]{1,0,2:T(4,128)(2,1)} %copy.10) | data formatting | bytes 7372800 | tf_op jit(solution)/shard_map/reshape | solution.py:39
  80.8 0.0 copy-start.1
  80.8 4.9 %fusion.32 = (bf16[89,128,160]{1,0,2:T(8,128)(2,1)S(1)}, bf16[89,128,160]{1,0,2:T(8,128)(2,1)S(1)}) fusion(bf16[90,128,160]{1,0,2:T(8,128)(2,1)} %reshape.24), kind=kLoop, calls=%fused_computation.44 | loop fusion | bytes 14581760 | tf_op jit(solution)/shard_map/slice | solution.py:40
  85.8 0.0 copy-done.1
  85.8 3.7 %multiply_convert_fusion.2 = bf16[64,89,160]{1,0,2:T(8,128)(2,1)S(1)} fusion(f32[160]{0:T(256)S(1)} %multiply_sqrt_fusion, bf16[89,128,160]{1,0,2:T(8,128)(2,1)S(1)} %get-tuple-element.8, bf16[89,128,160]{1,0,2:T(8,128)(2,1)S(1)} %get-tuple-element.7, s32[64]{0:T(128)S(1)} %copy-done.1, f32[256]{0:T(256)S(1)} %fusion.21), kind=kOutput, calls=%fused_computation.7 | convolution fusion | flops 483282944 | bytes 9115520 | tf_op jit(solution)/shard_map/fn,bnp->fbp/dot_general | solution.py:41
  89.4 3.6 %multiply_convert_fusion.1 = bf16[64,89,160]{1,0,2:T(8,128)(2,1)S(1)} fusion(f32[160]{0:T(256)S(1)} %multiply_sqrt_fusion, bf16[89,128,160]{1,0,2:T(8,128)(2,1)S(1)} %get-tuple-element.8, bf16[89,128,160]{1,0,2:T(8,128)(2,1)S(1)} %get-tuple-element.7, f32[256]{0:T(256)S(1)} %fusion.20, s32[64]{0:T(128)S(1)} %copy-done.1), kind=kOutput, calls=%fused_computation.6 | convolution fusion | flops 483282944 | bytes 9115520 | tf_op jit(solution)/shard_map/fn,bnp->fbp/dot_general | solution.py:42
  93.1 2.2 pad_maximum_fusion.2
  95.3 17.2 %fusion = f32[64,178,178]{2,1,0:T(8,128)} fusion(bf16[64,178,160]{1,0,2:T(8,128)(2,1)S(1)} %pad_maximum_fusion.2), kind=kOutput, calls=%fused_computation.4 | convolution fusion | flops 648888320 | bytes 11756544 | tf_op jit(solution)/shard_map/fip,fjp->fij/dot_general | solution.py:23
  112.5 9.8 %fusion.5 = (f32[64,1,89,89]{3,2,0,1:T(8,128)S(1)}, f32[64,1,89,89]{3,2,0,1:T(8,128)}) fusion(f32[64,178,178]{2,1,0:T(8,128)} %fusion), kind=kLoop, calls=%fused_computation.13 | loop fusion | flops 1013888 | bytes 12166656 | tf_op jit(solution)/shard_map/stack | solution.py:26
  122.3 2.6 pad_maximum_fusion.1
  124.9 7.8 %copy.13 = f32[64,2,89,89]{3,1,2,0:T(2,128)} copy(f32[64,2,89,89]{3,2,0,1:T(8,128)S(1)} %pad_maximum_fusion.1) | data formatting | bytes 8111104 | tf_op jit(solution)/shard_map/stack | solution.py:26
  132.7 0.0 copy-start.2
  132.7 0.0 all-reduce.6.cloned.1.call-update
  132.7 0.0 all-reduce.4.cloned.1.call-start
  132.8 0.6 copy-done.2
  133.4 0.6 dynamic-slice
  134.6 126.2 %all-reduce.6.cloned.1.call-done = f32[64,2,89,89]{3,1,2,0:T(2,128)} async-done(((f32[64,2,89,89]{3,1,2,0:T(2,128)}), f32[64,2,89,89]{3,1,2,0:T(2,128)}) %all-reduce.6.cloned.1.call-update) | async-done | bytes 4055568
  260.8 2.0 constant_dynamic-slice_fusion
  262.8 0.0 all-reduce.4.cloned.1.call-update
  262.8 49.2 %all-reduce.4.cloned.1.call-done = f32[8,2,89,89]{3,1,2,0:T(2,128)} async-done(((f32[8,2,89,89]{3,1,2,0:T(2,128)}), f32[8,2,89,89]{3,1,2,0:T(2,128)}) %all-reduce.4.cloned.1.call-update) | async-done | bytes 506960 | tf_op jit(solution)/shard_map/psum | solution.py:49
  312.0 2.0 copy.18
  (2 shorter events, 0.1 us)
Async XLA Ops:
  6.5 6.2 %copy-start = (f32[2880]{0:T(1024)S(1)}, f32[2880]{0:T(1024)}, u32[]{:S(2)}) copy-start(f32[2880]{0:T(1024)} %param.5) | copy-start | bytes 34564
  17.3 49.1 %all-to-all-start = ((bf16[2880,4,160]{0,2,1:T(8,128)(2,1)}), bf16[2880,4,160]{0,2,1:T(8,128)(2,1)}, u32[]{:S(2)}, u32[]{:S(2)}) async-start(bf16[2880,4,160]{0,2,1:T(8,128)(2,1)} %bitcast.15), calls=%async_computation | async-start | bytes 7536640 | tf_op jit(solution)/shard_map/all_to_all | solution.py:31
  22.5 238.3 %all-reduce.6.cloned.1.call-start = ((), (), s32[]{:S(2)}) async-start(), calls=%async_computation.2 | async-start | bytes 11665408
  80.8 4.9 %copy-start.1 = (s32[64]{0:T(128)S(1)}, s32[64]{0:T(128)}, u32[]{:S(2)}) copy-start(s32[64]{0:T(128)} %param.7) | copy-start | bytes 772
  132.7 0.7 copy-start.2
  132.7 179.3 %all-reduce.4.cloned.1.call-start = ((), (), s32[]{:S(2)}) async-start(), calls=%async_computation.1 | async-start | bytes 1458176 | tf_op jit(solution)/shard_map/psum | solution.py:49
Sparse Core Ops, SparseCore 0:
  132.9 127.8 all-reduce.5
  263.9 48.1 all-reduce.3
where the time goes:
time: 322 us; the launch traced here: 321 us
  waiting for transfers between devices  219 us (68%)
  local copies, waits for them, and re-layouts  38.5 us (12%)
  matrix products  24.5 us (8%)
  other arithmetic  20.1 us (6%)
  between operations  14.1 us (4%)
  starting transfers between devices  5.21 us (2%)
    unnamed x3, waiting for transfers between devices  126 us
    psum x1, waiting for transfers between devices, per_device(): return lax.psum(partial_value, 'tm')  49.2 us
    all_to_all x1, waiting for transfers between devices, per_device(): lax.all_to_all(values, 'tm', split_axis=1, concat_axis=0, tiled=True)  43.1 us
    dot_general x1, matrix products, cross_matrices(): jnp.einsum('fip,fjp->fij', stacked, stacked, preferred_element_type=jnp.f...  17.2 us
    another operation x2, other arithmetic, cross_matrices(): return jnp.stack([matrix_re, matrix_im], axis=1)  12.4 us
    unnamed x10, local copies, waits for them, and re-layouts  11.4 us
    reshape x1, local copies, waits for them, and re-layouts, per_device(): hop_rows = regrouped.reshape(-1, NFFT // 2, point_count)  8.52 us
    another operation x1, local copies, waits for them, and re-layouts, cross_matrices(): return jnp.stack([matrix_re, matrix_im], axis=1)  7.81 us
  transfers between devices with their start and end apart: 3, of which 3 were waited for; matrix products, arithmetic and copies ran while one was open for 0% of the time, Pallas kernels for 0%

commit v1 on v0

--- a/solution.py
+++ b/solution.py
@@ -1,11 +1,19 @@
+import functools
 import math
 
 import jax
 import jax.numpy as jnp
 from jax import lax
+from jax.experimental import pallas as pl
+from jax.experimental.pallas import tpu as pltpu
 from jax.sharding import PartitionSpec as P
 
 NFFT = 256
+HOP = NFFT // 2
+HALO = 192
+SLOTS = 24
+LANES = 128
+MESH = pl.DeviceIdType.MESH
 
 
 def make_tables(freq_indices):
@@ -18,6 +26,241 @@
     return (cosine_table, sine_table)
 
 
+def block_ranges(rows, nt):
+    blocks = rows * nt // HOP - 1
+    firsts = [-(-t * rows // HOP) for t in range(nt)] + [blocks]
+    return [(firsts[t], min(firsts[t + 1], blocks) - firsts[t]) for t in range(nt)]
+
+
+def kernel(
+    nt, nz, chunks, ranges, total_points,
+    codes_ref, scales_ref, weights_ref, table_ref, out_ref,
+    vals, stage, send, recv, part, corebuf, summed, zbuf, gath,
+    halo_s, halo_r, tm_s, tm_r, core_s, core_r, z_s, z_r, g_s, g_r,
+):
+    rows, points = codes_ref.shape
+    t = lax.axis_index("tm")
+    p = lax.axis_index("pts")
+    z = p // 2
+    c = p % 2
+    partner = p + 1 - 2 * c
+    per = 2 * nz
+    lane_tiles = points // LANES
+
+    barrier = pltpu.get_barrier_semaphore()
+    for d in range(1, nt):
+        pl.semaphore_signal(barrier, inc=1, device_id=((t + d) % nt, p), device_id_type=MESH)
+    pl.semaphore_signal(barrier, inc=1, device_id=(t, partner), device_id_type=MESH)
+    for d in range(1, nz):
+        pl.semaphore_signal(barrier, inc=1, device_id=(t, (z + d) % nz * 2 + c), device_id_type=MESH)
+
+    step = HALO // 2
+
+    def dequantize(i, carry):
+        at = pl.ds(pl.multiple_of(i * step, step), step)
+        vals[at, :] = (codes_ref[at, :].astype(jnp.float32) * scales_ref[at, :]).astype(jnp.bfloat16)
+        return carry
+
+    lax.fori_loop(0, HALO // step, dequantize, 0)
+    pl.semaphore_wait(barrier, nt + nz - 1)
+    halo = pltpu.make_async_remote_copy(
+        src_ref=vals.at[pl.ds(0, HALO)],
+        dst_ref=vals.at[pl.ds(rows, HALO)],
+        send_sem=halo_s, recv_sem=halo_r,
+        device_id=((t + nt - 1) % nt, p), device_id_type=MESH,
+    )
+    halo.start()
+    tail = vals.shape[0] - rows - HALO
+    vals[pl.ds(rows + HALO, tail), :] = jnp.zeros((tail, points), jnp.bfloat16)
+    lax.fori_loop(HALO // step, rows // step, dequantize, 0)
+
+    offset = (t % 2) * (HOP // 2)
+    root_weight = jnp.sqrt(weights_ref[...] / total_points)
+    table_rows = table_ref.shape[1]
+    used = max(count for _, count in ranges)
+    for lane in range(lane_tiles):
+        for spare in range(used, SLOTS):
+            stage[lane, pl.ds(spare, table_rows, stride=SLOTS), :] = jnp.zeros((table_rows, LANES), jnp.float32)
+
+    def exchange(k, d):
+        return pltpu.make_async_remote_copy(
+            src_ref=send.at[k, d - 1],
+            dst_ref=recv.at[k, :, t],
+            send_sem=tm_s.at[k, d - 1], recv_sem=tm_r.at[k, d - 1],
+            device_id=((t + d) % nt, p), device_id_type=MESH,
+        )
+
+    safe = (rows - HOP // 2 - NFFT) // HOP + 1
+    for k in range(chunks):
+        table = table_ref[k]
+
+        def spectrum(i, carry):
+            window = vals[pl.ds(pl.multiple_of(offset + i * HOP, HOP // 2), NFFT), :]
+            result = jnp.dot(table, window, preferred_element_type=jnp.float32) * root_weight
+            for lane in range(lane_tiles):
+                stage[lane, pl.ds(i, table_rows, stride=SLOTS), :] = result[:, lane * LANES:(lane + 1) * LANES]
+            return carry
+
+        lax.fori_loop(0, safe, spectrum, 0)
+        if k == 0:
+            halo.wait()
+        lax.fori_loop(safe, used, spectrum, 0)
+
+        for d in (3, 1, 2, 0):
+            dest = (t + d) % nt
+
+            def pack(f, carry):
+                base = pl.multiple_of((dest * per + f) * 2 * SLOTS, 2 * SLOTS)
+                for lane in range(lane_tiles):
+                    block = stage[lane, pl.ds(base, 2 * SLOTS), :].astype(jnp.bfloat16)
+                    at = slice(lane * LANES, (lane + 1) * LANES)
+                    if d == 0:
+                        recv[k, f, t, :, at] = block
+                    else:
+                        send[k, d - 1, f, :, at] = block
+                return carry
+
+            lax.fori_loop(0, per, pack, 0)
+            if d:
+                exchange(k, d).start()
+
+    width = nt * 2 * SLOTS
+    wide = 2 * LANES
+    lane_in = lax.broadcasted_iota(jnp.int32, (1, wide), 1) % (2 * SLOTS) < SLOTS
+    sign = jnp.where(lane_in, -1.0, 1.0)
+
+    def to_core(k):
+        return pltpu.make_async_remote_copy(
+            src_ref=part.at[k, :, 1 - c], dst_ref=corebuf.at[k],
+            send_sem=core_s.at[k], recv_sem=core_r.at[k],
+            device_id=(t, partner), device_id_type=MESH,
+        )
+
+    def to_z(k, d):
+        return pltpu.make_async_remote_copy(
+            src_ref=summed.at[k, (z + d) % nz], dst_ref=zbuf.at[k, d - 1],
+            send_sem=z_s.at[k, d - 1], recv_sem=z_r.at[k, d - 1],
+            device_id=(t, (z + d) % nz * 2 + c), device_id_type=MESH,
+        )
+
+    def to_tm(k, d):
+        return pltpu.make_async_remote_copy(
+            src_ref=gath.at[t, k], dst_ref=gath.at[t, k],
+            send_sem=g_s.at[k, d - 1], recv_sem=g_r.at[k, d - 1],
+            device_id=((t + d) % nt, p), device_id_type=MESH,
+        )
+
+    for k in range(chunks):
+        for d in range(1, nt):
+            exchange(k, d).wait()
+
+        def cross(f, carry):
+            stacked = recv[k, f].reshape(width, points)
+            prod = lax.dot_general(
+                stacked, stacked, (((1,), (1,)), ((), ())), preferred_element_type=jnp.float32
+            )
+            real = jnp.concatenate(
+                [prod[2 * s * SLOTS:(2 * s + 1) * SLOTS] for s in range(nt)], axis=0)
+            imag = jnp.concatenate(
+                [prod[(2 * s + 1) * SLOTS:(2 * s + 2) * SLOTS] for s in range(nt)], axis=0)
+            fill = jnp.zeros((nt * SLOTS, wide - width), jnp.float32)
+            real = jnp.concatenate([real, fill], axis=1)
+            imag = jnp.concatenate([imag, fill], axis=1)
+            both = real + sign * imag
+            both = both + pltpu.roll(both, wide - SLOTS, 1)
+            moved = pltpu.roll(both, wide - 3 * SLOTS, 1)
+            part[k, f // 2, f % 2] = jnp.where(lane_in[:, :LANES], both[:, :LANES], moved[:, :LANES])
+            return carry
+
+        lax.fori_loop(0, per, cross, 0)
+        to_core(k).start()
+        to_core(k).wait()
+        summed[k] = part[k, :, c] + corebuf[k]
+        for d in range(1, nz):
+            to_z(k, d).start()
+
+    for k in range(chunks):
+        for d in range(1, nz):
+            to_z(k, d).wait()
+        total = summed[k, z]
+        for d in range(1, nz):
+            total = total + zbuf[k, d - 1]
+        gath[t, k] = total
+        for d in range(1, nt):
+            to_tm(k, d).start()
+
+    for k in range(chunks):
+        for d in range(1, nt):
+            to_tm(k, d).wait()
+
+    places = [0, 2, 1, 3]
+    column = lax.broadcasted_iota(jnp.int32, (1, LANES), 1)
+
+    def finish(i, carry):
+        s = i // chunks
+        k = i % chunks
+        packed = gath[s, k]
+        placed = packed
+        for g in range(1, nt):
+            shift = (ranges[g][0] - places[g] * SLOTS) % LANES
+            placed = jnp.where(column >= ranges[g][0], pltpu.roll(packed, shift, 1), placed)
+        ordered = jnp.concatenate(
+            [placed[g * SLOTS:g * SLOTS + ranges[g][1]] for g in range(nt)]
+            + [jnp.zeros((LANES - sum(n for _, n in ranges), LANES), jnp.float32)], axis=0)
+        mirrored = ordered.T
+        keep = out_ref.shape[2]
+        out_ref[i, 0] = (0.5 * (ordered + mirrored))[:keep]
+        out_ref[i, 1] = (0.5 * (ordered - mirrored))[:keep]
+        return carry
+
+    lax.fori_loop(0, nt * chunks, finish, 0)
+
+
+def fused(nt, np_, codes, scales, weights, freq_indices):
+    rows, points = codes.shape
+    nf = freq_indices.shape[0]
+    nz = np_ // 2
+    chunks = nf // (nt * np_)
+    ranges = block_ranges(rows, nt)
+    blocks = rows * nt // HOP - 1
+    order = freq_indices.reshape(np_, nt, chunks).transpose(2, 1, 0).reshape(-1)
+    cosine_table, sine_table = make_tables(order)
+    table = jnp.stack([cosine_table, sine_table], axis=1).reshape(chunks, 2 * nt * np_, NFFT)
+    height = nt * SLOTS
+    used = max(count for _, count in ranges)
+    vals_rows = HOP // 2 + (used - 1) * HOP + NFFT
+    f32, bf16 = jnp.float32, jnp.bfloat16
+    dma = pltpu.SemaphoreType.DMA
+    vmem = pl.BlockSpec(memory_space=pltpu.VMEM)
+    full = pl.pallas_call(
+        functools.partial(kernel, nt, nz, chunks, ranges, points * np_),
+        out_shape=jax.ShapeDtypeStruct((nt * chunks, 2, height, LANES), f32),
+        in_specs=[vmem] * 4,
+        out_specs=vmem,
+        scratch_shapes=[
+            pltpu.VMEM((vals_rows, points), bf16),
+            pltpu.VMEM((points // LANES, 2 * nt * np_ * SLOTS, LANES), f32),
+            pltpu.VMEM((chunks, nt - 1, np_, 2 * SLOTS, points), bf16),
+            pltpu.VMEM((chunks, np_, nt, 2 * SLOTS, points), bf16),
+            pltpu.VMEM((chunks, nz, 2, height, LANES), f32),
+            pltpu.VMEM((chunks, nz, height, LANES), f32),
+            pltpu.VMEM((chunks, nz, height, LANES), f32),
+            pltpu.VMEM((chunks, nz - 1, height, LANES), f32),
+            pltpu.VMEM((nt, chunks, height, LANES), f32),
+            dma, dma,
+            dma((chunks, nt - 1)), dma((chunks, nt - 1)),
+            dma((chunks,)), dma((chunks,)),
+            dma((chunks, nz - 1)), dma((chunks, nz - 1)),
+            dma((chunks, nt - 1)), dma((chunks, nt - 1)),
+        ],
+        compiler_params=pltpu.CompilerParams(
+            collective_id=0, has_side_effects=True, vmem_limit_bytes=48 * 2**20
+        ),
+        name="spectra_cross",
+    )(codes, scales.reshape(-1, 1), weights.reshape(1, -1), table)
+    return full[:, :, :blocks, :blocks]
+
+
 def cross_matrices(stacked):
     blocks = stacked.shape[1] // 2
     products = jnp.einsum("fip,fjp->fij", stacked, stacked, preferred_element_type=jnp.float32)
@@ -26,7 +269,7 @@
     return jnp.stack([matrix_re, matrix_im], axis=1)
 
 
-def per_device(codes, scales, weights, freq_indices):
+def general(codes, scales, weights, freq_indices):
     values = (codes.astype(jnp.float32) * scales[:, None]).astype(jnp.bfloat16)
     regrouped = lax.all_to_all(values, "tm", split_axis=1, concat_axis=0, tiled=True)
     point_count = regrouped.shape[1]
@@ -50,6 +293,23 @@
 
 
 def solution(mesh):
+    nt, np_ = mesh.shape["tm"], mesh.shape["pts"]
+
+    def per_device(codes, scales, weights, freq_indices):
+        rows, points = codes.shape
+        fits = (
+            nt == 4
+            and np_ == 8
+            and freq_indices.shape[0] % (nt * np_) == 0
+            and points % LANES == 0
+            and rows % HALO == 0
+            and rows % HOP == HOP // 2
+            and max(count for _, count in block_ranges(rows, nt)) <= SLOTS
+        )
+        if fits:
+            return fused(nt, np_, codes, scales, weights, freq_indices)
+        return general(codes, scales, weights, freq_indices)
+
     return jax.shard_map(
         per_device,
         mesh=mesh,

time: 322 us -> 79 us (0.25)
  waiting for transfers between devices: 219 us -> 0 us
  Pallas kernels: 0 us -> 71.9 us
  local copies, waits for them, and re-layouts: 38.5 us -> 6.36 us
  matrix products: 24.5 us -> 0 us
  other arithmetic: 20.1 us -> 0.42 us
  between operations: 14.1 us -> 0.06 us
  starting transfers between devices: 5.21 us -> 0 us
    unnamed x3 -> x0, waiting for transfers between devices: 126 us -> none
    pallas_call x0 -> x1, Pallas kernels: none -> 71.9 us  [fused(): pl.pallas_call(functools.partial(kernel, nt, nz, chunks, ranges, points *...]
    psum x1 -> x0, waiting for transfers between devices: 49.2 us -> none  [per_device(): return lax.psum(partial_value, 'tm')]
    all_to_all x1 -> x0, waiting for transfers between devices: 43.1 us -> none  [per_device(): lax.all_to_all(values, 'tm', split_axis=1, concat_axis=0, tiled=True)]
    dot_general x3 -> x0, matrix products: 24.5 us -> none  [the longest x1 17.2 us: cross_matrices(): jnp.einsum('fip,fjp->fij', stacked, stacked, preferred_element_type=jnp.f...]
    another operation x2 -> x1, other arithmetic: 12.4 us -> 0.01 us  [fused(): jnp.stack([cosine_table, sine_table], axis=1)]
    unnamed x10 -> x2, local copies, waits for them, and re-layouts: 11.4 us -> 2.04 us
    another operation x1, local copies, waits for them, and re-layouts: 7.81 us -> 0.07 us  [fused(): jnp.stack([cosine_table, sine_table], axis=1)]
  transfers between devices with their start and end apart: 3 -> 0, of which waited for: 3 -> 0; matrix products, arithmetic and copies ran while one was open for 0% -> 0% of each run, Pallas kernels for 0% -> 0%
where the time goes in v1:
time: 79 us; the launch traced here: 78.7 us
  Pallas kernels  71.9 us (91%)
  local copies, waits for them, and re-layouts  6.36 us (8%)
    pallas_call x1, Pallas kernels, fused(): pl.pallas_call(functools.partial(kernel, nt, nz, chunks, ranges, points *...  71.9 us
    unnamed x2, local copies, waits for them, and re-layouts  2.04 us

profile of v1, /device:TPU:0, one launch (start us, length us, event | category | flops | bytes accessed | tf_op | source)
XLA Modules:
  0.0 78.7 jit_solution(13558466599439691470)
XLA Ops:
  0.0 0.7 reshape.189.weights_ref
  0.7 0.8 reshape.190
  1.5 0.1 copy.10
  1.6 0.1 mul.128
  1.7 0.4 multiply_convert_fusion.1
  2.1 0.1 copy.11
  2.2 1.1 %reshape.192.scales_ref = f32[2880,1]{1,0:T(8,128)S(1)} reshape(f32[2880]{0:T(1024)} %param.5) | data formatting | bytes 23040 | tf_op jit(solution)/shard_map/reshape | solution.py:260
  3.3 0.0 copy-start
  3.4 2.0 %copy-done = bf16[2880,640]{1,0:T(8,128)(2,1)S(1)} copy-done((bf16[2880,640]{1,0:T(8,128)(2,1)S(1)}, bf16[2880,640]{1,0:T(8,128)(2,1)}, u32[]{:S(2)}) %copy-start) | copy-done | bytes 3686424
  5.4 71.9 %spectra_cross.1 = f32[8,2,96,128]{3,2,1,0:T(8,128)S(1)} custom-call(bf16[2880,640]{1,0:T(8,128)(2,1)S(1)} %copy-done, f32[2880,1]{1,0:T(8,128)S(1)} %reshape.192.scales_ref, f32[1,640]{1,0:T(1,128)S(1)} %reshape.189.weights_ref, bf16[2,64,256]{2,1,0:T(8,128)(2,1)S(1)} %reshape.191.table_ref), custom_call_target="tpu_custom_call" | custom-call | tf_op jit(solution)/shard_map/spectra_cross/pallas_call | solution.py:235
  77.3 1.4 %copy.13 = f32[8,2,89,89]{3,1,2,0:T(2,128)} copy(f32[8,2,89,89]{3,2,1,0:T(8,128)S(1)} %bitcast.2) | data formatting | bytes 1013888 | tf_op jit(solution)/shard_map/slice | solution.py:261
  (3 shorter events, 0.1 us)
Async XLA Ops:
  3.3 2.0 %copy-start = (bf16[2880,640]{1,0:T(8,128)(2,1)S(1)}, bf16[2880,640]{1,0:T(8,128)(2,1)}, u32[]{:S(2)}) copy-start(bf16[2880,640]{1,0:T(8,128)(2,1)} %codes_ref.1) | copy-start | bytes 11059204

commit v2 on v1

v2 whole, which is shorter than its diff:
```python
import functools
import math

import jax
import jax.numpy as jnp
from jax import lax
from jax.experimental import pallas as pl
from jax.experimental.pallas import tpu as pltpu
from jax.sharding import PartitionSpec as P

NFFT = 256
HOP = NFFT // 2
HALO = 192
SLOTS = 24
LANES = 128
MESH = pl.DeviceIdType.MESH


def make_tables(freq_indices):
    sample = jnp.arange(NFFT, dtype=jnp.int32)
    phases = freq_indices[:, None] * sample[None, :] % NFFT
    angles = phases.astype(jnp.float32) * (2.0 * math.pi / NFFT)
    hann_window = 0.5 - 0.5 * jnp.cos(sample.astype(jnp.float32) * (2.0 * math.pi / NFFT))
    cosine_table = (0.25 * hann_window[None, :] * jnp.cos(angles)).astype(jnp.bfloat16)
    sine_table = (-0.25 * hann_window[None, :] * jnp.sin(angles)).astype(jnp.bfloat16)
    return (cosine_table, sine_table)


def block_ranges(rows, nt):
    blocks = rows * nt // HOP - 1
    firsts = [-(-t * rows // HOP) for t in range(nt)] + [blocks]
    return [(firsts[t], min(firsts[t + 1], blocks) - firsts[t]) for t in range(nt)]


def kernel(
    nt, nz, chunks, ranges, total_points,
    codes_hbm, scales_ref, weights_ref, table_ref, out_ref,
    codes_ref, vals, stage, send, recv, part, corebuf, summed, zbuf, gath,
    load_s, halo_s, halo_r, tm_s, tm_r, core_s, core_r, z_s, z_r, g_s, g_r,
):
    rows, points = codes_ref.shape
    t = lax.axis_index("tm")
    p = lax.axis_index("pts")
    z = p // 2
    c = p % 2
    partner = p + 1 - 2 * c
    per = 2 * nz
    half = per // 2
    lane_tiles = points // LANES
    groups = SLOTS // 8
    used = max(count for _, count in ranges)
    step = HALO // 2

    ends = [
        min(-(-(HOP // 2 + (8 * g + 7) * HOP + NFFT) // step) * step, rows) for g in range(groups - 1)
    ] + [rows]
    starts = [0] + ends[:-1]
    loads = [
        pltpu.make_async_copy(
            codes_hbm.at[pl.ds(starts[g], ends[g] - starts[g])],
            codes_ref.at[pl.ds(starts[g], ends[g] - starts[g])],
            load_s.at[g],
        )
        for g in range(groups)
    ]
    for load in loads:
        load.start()

    barrier = pltpu.get_barrier_semaphore()
    for d in range(1, nt):
        pl.semaphore_signal(barrier, inc=1, device_id=((t + d) % nt, p), device_id_type=MESH)
    pl.semaphore_signal(barrier, inc=1, device_id=(t, partner), device_id_type=MESH)
    for d in range(1, nz):
        pl.semaphore_signal(barrier, inc=1, device_id=(t, (z + d) % nz * 2 + c), device_id_type=MESH)

    root_weight = jnp.sqrt(weights_ref[...] / total_points)
    tail = vals.shape[0] - rows - HALO
    vals[pl.ds(rows + HALO, tail), :] = jnp.zeros((tail, points), jnp.bfloat16)
    half_rows = table_ref.shape[1] // 2

    def place(i, lane, result):
        at = (i // 8) * 16 + i % 8
        for part_of in range(2):
            stage[lane, pl.ds(at + 8 * part_of, half_rows, stride=2 * SLOTS), :] = result[part_of]

    for lane in range(lane_tiles):
        for spare in range(used, SLOTS):
            place(spare, lane, [jnp.zeros((half_rows, LANES), jnp.float32)] * 2)

    def dequantize(i, carry):
        at = pl.ds(pl.multiple_of(i * step, step), step)
        vals[at, :] = (codes_ref[at, :].astype(jnp.float32) * scales_ref[at, :]).astype(jnp.bfloat16)
        return carry

    halo = pltpu.make_async_remote_copy(
        src_ref=vals.at[pl.ds(0, HALO)],
        dst_ref=vals.at[pl.ds(rows, HALO)],
        send_sem=halo_s, recv_sem=halo_r,
        device_id=((t + nt - 1) % nt, p), device_id_type=MESH,
    )
    offset = (t % 2) * (HOP // 2)

    def spectra(k, first, last):
        table = table_ref[k]

        def spectrum(i, carry):
            window = vals[pl.ds(pl.multiple_of(offset + i * HOP, HOP // 2), NFFT), :]
            result = jnp.dot(table, window, preferred_element_type=jnp.float32) * root_weight
            for lane in range(lane_tiles):
                columns = result[:, lane * LANES:(lane + 1) * LANES]
                place(i, lane, [columns[:half_rows], columns[half_rows:]])
            return carry

        lax.fori_loop(first, last, spectrum, 0)

    def pack_group(k, g, d):
        dest = (t + d) % nt

        def pack(f, carry):
            base = pl.multiple_of((dest * per + f) * 2 * SLOTS + g * 16, 16)
            for lane in range(lane_tiles):
                block = stage[lane, pl.ds(base, 16), :].astype(jnp.bfloat16)
                at = slice(lane * LANES, (lane + 1) * LANES)
                if d == 0:
                    recv[k, f, t, g * 16:(g + 1) * 16, at] = block
                else:
                    send[k, d - 1, f, g * 16:(g + 1) * 16, at] = block
            return carry

        lax.fori_loop(0, per, pack, 0)

    def exchange(k, piece, d):
        if k < chunks - 1:
            src = send.at[k, d - 1, :, pl.ds(piece * 16, 16)]
            dst = recv.at[k, :, t, pl.ds(piece * 16, 16)]
        else:
            src = send.at[k, d - 1, pl.ds(piece * half, half)]
            dst = recv.at[k, pl.ds(piece * half, half), t]
        return pltpu.make_async_remote_copy(
            src_ref=src, dst_ref=dst,
            send_sem=tm_s.at[k, piece, d - 1], recv_sem=tm_r.at[k, piece, d - 1],
            device_id=((t + d) % nt, p), device_id_type=MESH,
        )

    safe = (rows - HOP // 2 - NFFT) // HOP + 1
    partners = (3, 1, 2)
    for k in range(chunks):
        for g in range(groups):
            first, last = 8 * g, min(8 * g + 8, used)
            if k == 0:
                loads[g].wait()
                lax.fori_loop(starts[g] // step, ends[g] // step, dequantize, 0)
                if g == 0:
                    pl.semaphore_wait(barrier, nt + nz - 1)
                    halo.start()
                if last > safe:
                    spectra(k, first, safe)
                    halo.wait()
                    first = safe
            spectra(k, first, last)
            for d in partners + (0,):
                pack_group(k, g, d)
                if d and k < chunks - 1:
                    exchange(k, g, d).start()
        if k == chunks - 1:
            for h in range(2):
                for d in partners:
                    exchange(k, h, d).start()

    width = nt * 2 * SLOTS
    wide = 2 * LANES
    eights = nt * groups
    lane_in = lax.broadcasted_iota(jnp.int32, (1, wide), 1) % 16 < 8
    sign = jnp.where(lane_in, -1.0, 1.0)

    def to_core(k, h):
        at = pl.ds(h * nz // 2, nz // 2)
        return pltpu.make_async_remote_copy(
            src_ref=part.at[k, at, 1 - c], dst_ref=corebuf.at[k, at],
            send_sem=core_s.at[k, h], recv_sem=core_r.at[k, h],
            device_id=(t, partner), device_id_type=MESH,
        )

    def to_z(k, peer):
        return pltpu.make_async_remote_copy(
            src_ref=summed.at[k, peer], dst_ref=zbuf.at[k, z],
            send_sem=z_s.at[k, peer], recv_sem=z_r.at[k, z],
            device_id=(t, peer * 2 + c), device_id_type=MESH,
        )

    def from_z(k, peer):
        return pltpu.make_async_remote_copy(
            src_ref=summed.at[k, peer], dst_ref=zbuf.at[k, peer],
            send_sem=z_s.at[k, peer], recv_sem=z_r.at[k, peer],
            device_id=(t, peer * 2 + c), device_id_type=MESH,
        )

    def to_tm(k, d):
        return pltpu.make_async_remote_copy(
            src_ref=gath.at[t, k], dst_ref=gath.at[t, k],
            send_sem=g_s.at[k, d - 1], recv_sem=g_r.at[k, d - 1],
            device_id=((t + d) % nt, p), device_id_type=MESH,
        )

    def cross_half(k, h):
        def cross(f, carry):
            stacked = recv[k, f].reshape(width, points)
            prod = lax.dot_general(
                stacked, stacked, (((1,), (1,)), ((), ())), preferred_element_type=jnp.float32
            )
            real = jnp.concatenate([prod[16 * m:16 * m + 8] for m in range(eights)], axis=0)
            imag = jnp.concatenate([prod[16 * m + 8:16 * m + 16] for m in range(eights)], axis=0)
            fill = jnp.zeros((nt * SLOTS, wide - width), jnp.float32)
            real = jnp.concatenate([real, fill], axis=1)
            imag = jnp.concatenate([imag, fill], axis=1)
            both = real + sign * imag
            both = both + pltpu.roll(both, wide - 8, 1)
            moved = pltpu.roll(both, wide - (LANES - 8), 1)
            part[k, f // 2, f % 2] = jnp.where(lane_in[:, :LANES], both[:, :LANES], moved[:, :LANES])
            return carry

        lax.fori_loop(h * half, (h + 1) * half, cross, 0)
        to_core(k, h).start()
        to_core(k, h).wait()
        for peer in range(h * nz // 2, (h + 1) * nz // 2):
            summed[k, peer] = part[k, peer, c] + corebuf[k, peer]

            @pl.when(peer != z)
            def _():
                to_z(k, peer).start()

    def compress(padded):
        kept = [padded[s * SLOTS:s * SLOTS + ranges[s][1]] for s in range(nt)]
        fill = LANES - sum(n for _, n in ranges)
        return jnp.concatenate(kept + [jnp.zeros((fill, LANES), jnp.float32)], axis=0)

    def reduce_z(k):
        total = summed[k, z]
        for d in range(1, nz):
            peer = (z + d) % nz
            from_z(k, peer).wait()
            total = total + zbuf[k, peer]
        full = jnp.concatenate([total, jnp.zeros((LANES - nt * SLOTS, LANES), jnp.float32)], axis=0)
        turned = full.T
        where = [16 * m if m < 8 else 16 * (m - 8) + 8 for m in range(eights)]
        turned = jnp.concatenate([turned[w:w + 8] for w in where], axis=0)
        gath[t, k] = compress(compress(turned).T)[:nt * SLOTS]
        for d in range(1, nt):
            to_tm(k, d).start()

    def finish(k):
        for d in range(1, nt):
            to_tm(k, d).wait()

        def one(s, carry):
            ordered = gath[s, k]
            fill = jnp.zeros((LANES - nt * SLOTS, LANES), jnp.float32)
            mirrored = jnp.concatenate([ordered, fill], axis=0).T[:nt * SLOTS]
            out_ref[s * chunks + k, 0] = 0.5 * (ordered + mirrored)
            out_ref[s * chunks + k, 1] = 0.5 * (ordered - mirrored)
            return carry

        lax.fori_loop(0, nt, one, 0)

    for k in range(chunks):
        for h in range(2):
            if k == chunks - 1:
                for d in partners:
                    exchange(k, h, d).wait()
            elif h == 0:
                for g in range(groups):
                    for d in partners:
                        exchange(k, g, d).wait()
            cross_half(k, h)
        if k < chunks - 1:
            reduce_z(k)
    for k in range(chunks - 1):
        finish(k)
    reduce_z(chunks - 1)
    finish(chunks - 1)


def fused(nt, np_, codes, scales, weights, freq_indices):
    rows, points = codes.shape
    nf = freq_indices.shape[0]
    nz = np_ // 2
    chunks = nf // (nt * np_)
    ranges = block_ranges(rows, nt)
    blocks = rows * nt // HOP - 1
    order = freq_indices.reshape(np_, nt, chunks).transpose(2, 1, 0).reshape(-1)
    cosine_table, sine_table = make_tables(order)
    shape = (chunks, nt * np_, NFFT)
    table = jnp.concatenate([cosine_table.reshape(shape), sine_table.reshape(shape)], axis=1)
    height = nt * SLOTS
    used = max(count for _, count in ranges)
    vals_rows = HOP // 2 + (used - 1) * HOP + NFFT
    groups = SLOTS // 8
    f32, bf16 = jnp.float32, jnp.bfloat16
    dma = pltpu.SemaphoreType.DMA
    vmem = pl.BlockSpec(memory_space=pltpu.VMEM)
    full = pl.pallas_call(
        functools.partial(kernel, nt, nz, chunks, ranges, points * np_),
        out_shape=jax.ShapeDtypeStruct((nt * chunks, 2, height, LANES), f32),
        in_specs=[pl.BlockSpec(memory_space=pl.ANY)] + [vmem] * 3,
        out_specs=vmem,
        scratch_shapes=[
            pltpu.VMEM((rows, points), bf16),
            pltpu.VMEM((vals_rows, points), bf16),
            pltpu.VMEM((points // LANES, nt * np_ * 2 * SLOTS, LANES), f32),
            pltpu.VMEM((chunks, nt - 1, np_, 2 * SLOTS, points), bf16),
            pltpu.VMEM((chunks, np_, nt, 2 * SLOTS, points), bf16),
            pltpu.VMEM((chunks, nz, 2, height, LANES), f32),
            pltpu.VMEM((chunks, nz, height, LANES), f32),
            pltpu.VMEM((chunks, nz, height, LANES), f32),
            pltpu.VMEM((chunks, nz, height, LANES), f32),
            pltpu.VMEM((nt, chunks, height, LANES), f32),
            dma((groups,)),
            dma, dma,
            dma((chunks, groups, nt - 1)), dma((chunks, groups, nt - 1)),
            dma((chunks, 2)), dma((chunks, 2)),
            dma((chunks, nz)), dma((chunks, nz)),
            dma((chunks, nt - 1)), dma((chunks, nt - 1)),
        ],
        compiler_params=pltpu.CompilerParams(
            collective_id=0, has_side_effects=True, vmem_limit_bytes=60 * 2**20
        ),
        name="spectra_cross",
    )(codes, scales.reshape(-1, 1), weights.reshape(1, -1), table)
    return full[:, :, :blocks, :blocks]


def cross_matrices(stacked):
    blocks = stacked.shape[1] // 2
    products = jnp.einsum("fip,fjp->fij", stacked, stacked, preferred_element_type=jnp.float32)
    matrix_re = products[:, :blocks, :blocks] + products[:, blocks:, blocks:]
    matrix_im = products[:, :blocks, blocks:] - products[:, blocks:, :blocks]
    return jnp.stack([matrix_re, matrix_im], axis=1)


def general(codes, scales, weights, freq_indices):
    values = (codes.astype(jnp.float32) * scales[:, None]).astype(jnp.bfloat16)
    regrouped = lax.all_to_all(values, "tm", split_axis=1, concat_axis=0, tiled=True)
    point_count = regrouped.shape[1]
    own_weights = lax.dynamic_slice_in_dim(
        weights, lax.axis_index("tm") * point_count, point_count, 0
    )
    total_points = weights.shape[0] * lax.axis_size("pts")
    root_weight = jnp.sqrt(own_weights / total_points)
    cosine_table, sine_table = make_tables(freq_indices)
    hop_rows = regrouped.reshape(-1, NFFT // 2, point_count)
    windows = jnp.concatenate([hop_rows[:-1], hop_rows[1:]], axis=1)
    real_part = jnp.einsum("fn,bnp->fbp", cosine_table, windows, preferred_element_type=jnp.float32)
    imag_part = jnp.einsum("fn,bnp->fbp", sine_table, windows, preferred_element_type=jnp.float32)
    scaled_re = (real_part * root_weight[None, None, :]).astype(jnp.bfloat16)
    scaled_im = (imag_part * root_weight[None, None, :]).astype(jnp.bfloat16)
    stacked = jnp.concatenate([scaled_re, scaled_im], axis=1)
    partial_value = lax.psum_scatter(
        cross_matrices(stacked), "pts", scatter_dimension=0, tiled=True
    )
    return lax.psum(partial_value, "tm")


def solution(mesh):
    nt, np_ = mesh.shape["tm"], mesh.shape["pts"]

    def per_device(codes, scales, weights, freq_indices):
        rows, points = codes.shape
        fits = (
            nt == 4
            and np_ == 8
            and freq_indices.shape[0] % (nt * np_) == 0
            and points % LANES == 0
            and rows % HALO == 0
            and rows % HOP == HOP // 2
            and max(count for _, count in block_ranges(rows, nt)) <= SLOTS
        )
        if fits:
            return fused(nt, np_, codes, scales, weights, freq_indices)
        return general(codes, scales, weights, freq_indices)

    return jax.shard_map(
        per_device,
        mesh=mesh,
        in_specs=(P("tm", "pts"), P("tm"), P("pts"), P()),
        out_specs=P("pts", None, None, None),
        check_vma=False,
    )
```

time: 79 us -> 77.6 us (0.982)
  Pallas kernels: 71.9 us -> 68.8 us
    pallas_call x1, Pallas kernels: 71.9 us -> 68.8 us  [fused(): pl.pallas_call(functools.partial(kernel, nt, nz, chunks, ranges, points *...]
    unnamed x2 -> x0, local copies, waits for them, and re-layouts: 2.04 us -> none
    reshape x1, local copies, waits for them, and re-layouts: 1.14 us -> 2.29 us  [fused(): scales.reshape(-1, 1)]
    slice x1, local copies, waits for them, and re-layouts: 1.43 us -> 2.56 us  [fused(): return full[:, :, :blocks, :blocks]]
where the time goes in v2:
time: 77.6 us; the launch traced here: 76.9 us
  Pallas kernels  68.8 us (89%)
  local copies, waits for them, and re-layouts  7.07 us (9%)
  other arithmetic  1.04 us (1%)
    pallas_call x1, Pallas kernels, fused(): pl.pallas_call(functools.partial(kernel, nt, nz, chunks, ranges, points *...  68.8 us
    slice x1, local copies, waits for them, and re-layouts, fused(): return full[:, :, :blocks, :blocks]  2.56 us
    reshape x1, local copies, waits for them, and re-layouts, fused(): scales.reshape(-1, 1)  2.29 us

profile of v2, /device:TPU:0, one launch (start us, length us, event | category | flops | bytes accessed | tf_op | source)
XLA Modules:
  0.0 76.9 jit_solution(11725490098415203163)
XLA Ops:
  0.0 1.3 %reshape.53.weights_ref = f32[1,640]{1,0:T(1,128)} reshape(f32[640]{0:T(1024)} %param.6) | data formatting | bytes 5120 | tf_op jit(solution)/shard_map/reshape | solution.py:328
  1.3 0.8 reshape.54
  2.1 0.1 copy.7
  2.2 0.1 mul.98
  2.3 0.4 multiply_convert_fusion.1
  2.6 0.6 pad_maximum_fusion.table_ref
  3.3 2.3 %reshape.55.scales_ref = f32[2880,1]{1,0:T(8,128)} reshape(f32[2880]{0:T(1024)} %param.5) | data formatting | bytes 23040 | tf_op jit(solution)/shard_map/reshape | solution.py:328
  5.6 68.8 %spectra_cross.1 = f32[8,2,96,128]{3,2,1,0:T(8,128)} custom-call(bf16[2880,640]{1,0:T(8,128)(2,1)} %codes_hbm.1, f32[2880,1]{1,0:T(8,128)} %reshape.55.scales_ref, f32[1,640]{1,0:T(1,128)} %reshape.53.weights_ref, bf16[2,64,256]{2,1,0:T(8,128)(2,1)} %pad_maximum_fusion.table_ref), custom_call_target="tpu_custom_call" | custom-call | tf_op jit(solution)/shard_map/spectra_cross/pallas_call | solution.py:301
  74.4 2.6 %copy.9 = f32[8,2,89,89]{3,1,2,0:T(2,128)} copy(f32[8,2,89,89]{3,2,1,0:T(8,128)} %bitcast.2) | data formatting | bytes 1013888 | tf_op jit(solution)/shard_map/slice | solution.py:329
  (1 shorter events, 0.0 us)

commit v3 on v2

--- a/solution.py
+++ b/solution.py
@@ -322,7 +322,7 @@
             dma((chunks, nt - 1)), dma((chunks, nt - 1)),
         ],
         compiler_params=pltpu.CompilerParams(
-            collective_id=0, has_side_effects=True, vmem_limit_bytes=60 * 2**20
+            collective_id=0, has_side_effects=True, vmem_limit_bytes=52 * 2**20
         ),
         name="spectra_cross",
     )(codes, scales.reshape(-1, 1), weights.reshape(1, -1), table)

time: 77.6 us -> 74.4 us (0.959)
  local copies, waits for them, and re-layouts: 7.07 us -> 5.36 us
  Pallas kernels: 68.8 us -> 67.9 us
    slice x1, local copies, waits for them, and re-layouts: 2.56 us -> 1.43 us  [fused(): return full[:, :, :blocks, :blocks]]
    pallas_call x1, Pallas kernels: 68.8 us -> 67.9 us  [fused(): pl.pallas_call(functools.partial(kernel, nt, nz, chunks, ranges, points *...]
where the time goes in v3:
time: 74.4 us; the launch traced here: 73.7 us
  Pallas kernels  67.9 us (91%)
  local copies, waits for them, and re-layouts  5.36 us (7%)
    pallas_call x1, Pallas kernels, fused(): pl.pallas_call(functools.partial(kernel, nt, nz, chunks, ranges, points *...  67.9 us
    reshape x1, local copies, waits for them, and re-layouts, fused(): scales.reshape(-1, 1)  2.29 us

profile of v3, /device:TPU:0, one launch (start us, length us, event | category | flops | bytes accessed | tf_op | source)
XLA Modules:
  0.0 73.7 jit_solution(2303316703689081435)
XLA Ops:
  0.0 0.7 reshape.53.weights_ref
  0.7 0.8 %reshape.54 = s32[8,4,2]{2,1,0:T(4,128)S(1)} reshape(s32[64]{0:T(128)} %param.7) | data formatting | bytes 512 | tf_op jit(solution)/shard_map/reshape | solution.py:290
  1.5 0.1 copy.7
  1.6 0.1 mul.98
  1.7 0.4 multiply_convert_fusion.1
  2.1 2.3 %reshape.55.scales_ref = f32[2880,1]{1,0:T(8,128)} reshape(f32[2880]{0:T(1024)} %param.5) | data formatting | bytes 23040 | tf_op jit(solution)/shard_map/reshape | solution.py:328
  4.4 67.9 %spectra_cross.1 = f32[8,2,96,128]{3,2,1,0:T(8,128)S(1)} custom-call(bf16[2880,640]{1,0:T(8,128)(2,1)} %codes_hbm.1, f32[2880,1]{1,0:T(8,128)} %reshape.55.scales_ref, f32[1,640]{1,0:T(1,128)S(1)} %reshape.53.weights_ref, bf16[2,64,256]{2,1,0:T(8,128)(2,1)S(1)} %pad_maximum_fusion.table_ref), custom_call_target="tpu_custom_call" | custom-call | tf_op jit(solution)/shard_map/spectra_cross/pallas_call | solution.py:301
  72.3 1.4 %copy.9 = f32[8,2,89,89]{3,1,2,0:T(2,128)} copy(f32[8,2,89,89]{3,2,1,0:T(8,128)S(1)} %bitcast.2) | data formatting | bytes 1013888 | tf_op jit(solution)/shard_map/slice | solution.py:329
  (2 shorter events, 0.1 us)

commit v4 on v3

--- a/solution.py
+++ b/solution.py
@@ -73,7 +73,7 @@
     for d in range(1, nz):
         pl.semaphore_signal(barrier, inc=1, device_id=(t, (z + d) % nz * 2 + c), device_id_type=MESH)
 
-    root_weight = jnp.sqrt(weights_ref[...] / total_points)
+    root_weight = jnp.sqrt(weights_ref[...] / total_points).reshape(1, points)
     tail = vals.shape[0] - rows - HALO
     vals[pl.ds(rows + HALO, tail), :] = jnp.zeros((tail, points), jnp.bfloat16)
     half_rows = table_ref.shape[1] // 2
@@ -325,7 +325,7 @@
             collective_id=0, has_side_effects=True, vmem_limit_bytes=52 * 2**20
         ),
         name="spectra_cross",
-    )(codes, scales.reshape(-1, 1), weights.reshape(1, -1), table)
+    )(codes, scales.reshape(-1, 1), weights, table)
     return full[:, :, :blocks, :blocks]
 
 

time: 74.4 us -> 74.4 us (level)
  no operation moved by 1% of the time
where the time goes in v4:
time: 74.4 us; the launch traced here: 73.7 us
  Pallas kernels  67.9 us (91%)
  local copies, waits for them, and re-layouts  5.35 us (7%)
    pallas_call x1, Pallas kernels, fused(): pl.pallas_call(functools.partial(kernel, nt, nz, chunks, ranges, points *...  67.9 us
    reshape x1, local copies, waits for them, and re-layouts, fused(): scales.reshape(-1, 1)  2.29 us

profile of v4, /device:TPU:0, one launch (start us, length us, event | category | flops | bytes accessed | tf_op | source)
XLA Modules:
  0.0 73.7 jit_solution(1296904200524699564)
XLA Ops:
  0.0 0.8 %reshape.50 = s32[8,4,2]{2,1,0:T(4,128)S(1)} reshape(s32[64]{0:T(128)} %param.7) | data formatting | bytes 512 | tf_op jit(solution)/shard_map/reshape | solution.py:290
  0.8 0.1 copy.7
  0.9 0.1 mul.98
  1.0 0.4 multiply_convert_fusion.1
  1.4 2.3 %reshape.51.scales_ref = f32[2880,1]{1,0:T(8,128)} reshape(f32[2880]{0:T(1024)} %param.5) | data formatting | bytes 23040 | tf_op jit(solution)/shard_map/reshape | solution.py:328
  3.7 0.0 copy-start
  3.7 0.7 copy-done
  4.4 67.9 %spectra_cross.1 = f32[8,2,96,128]{3,2,1,0:T(8,128)S(1)} custom-call(bf16[2880,640]{1,0:T(8,128)(2,1)} %codes_hbm.1, f32[2880,1]{1,0:T(8,128)} %reshape.51.scales_ref, f32[640]{0:T(1024)S(1)} %copy-done, bf16[2,64,256]{2,1,0:T(8,128)(2,1)S(1)} %pad_maximum_fusion.table_ref), custom_call_target="tpu_custom_call" | custom-call | tf_op jit(solution)/shard_map/spectra_cross/pallas_call | solution.py:301
  72.3 1.4 %copy.9 = f32[8,2,89,89]{3,1,2,0:T(2,128)} copy(f32[8,2,89,89]{3,2,1,0:T(8,128)S(1)} %bitcast.2) | data formatting | bytes 1013888 | tf_op jit(solution)/shard_map/slice | solution.py:329
  (2 shorter events, 0.1 us)
Async XLA Ops:
  3.7 0.7 copy-start
